TPU v7x, 512 devices: a whole 4x8x8 slice. The times are simulated.
512 devices in a mesh: sec: 2 (over core), grp: 16 (over y_hi, x), dev: 16 (over y_lo, z).
Axes of the slice: x: 4, y: 8 (y_hi: 4, y_lo: 2; y = y_hi * 2 + y_lo), z: 8, core: 2. Of those that a mesh axis runs over, the one named last changes fastest.
Arguments:
- q_latent: bfloat16 [256, 128, 512], P(('grp', 'dev')), may hold values from -16 to 16
- q_rope: bfloat16 [256, 8192], P(('grp', 'dev')), may hold values from -6 to 6
- cache_latent: bfloat16 [256, 2048, 512], P(('grp', 'dev'), 'sec'), may hold values from -6 to 6
- cache_rope: bfloat16 [256, 64, 2048], P(('grp', 'dev'), None, 'sec'), may hold values from -6 to 6
- lengths: int32 [256], P(('grp', 'dev')), may hold values from 2 to 2048
- w_uv: bfloat16 [128, 512, 128], P(('sec', 'grp')), may hold values from -1 to 1
- w_out: bfloat16 [16384, 7168], P(('sec', 'grp'), 'dev'), may hold values from -0.046875 to 0.046875
- resid: bfloat16 [256, 7168], P(('sec', 'grp'), 'dev'), may hold values from -6 to 6
- norm_gain: float32 [7168], P('dev'), may hold values from 0.1 to 1.9
- router: float32 [7168, 16], P('dev'), may hold values from -0.0625 to 0.0625
- routes: int32 [256, 8], P(('sec', 'grp')), may hold values from 0 to 15, as said below
- slots: int32 [256, 8], P(('sec', 'grp')), may hold values from 0 to 7, as said below
- w_gateup: bfloat16 [16, 7168, 2, 2048], P('grp', 'dev', None, 'sec'), may hold values from -0.0625 to 0.0625
- w_down: bfloat16 [16, 2048, 7168], P('grp', 'sec', 'dev'), may hold values from -0.125 to 0.125
Outputs:
- layer_out: bfloat16 [256, 7168], P(('sec', 'grp'), 'dev')
Inputs may be any that keep to these rules, and one draw needn't show every extreme that they name: `routes`: each row names 8 different experts; one expert is named by every row. Within each aligned block of 8 rows, the routes that name one expert hold the slots 0, 1, ... up to their number less one, each once.
All inputs are finite; a program needn't handle non-finite values.
Results may differ from a plain program's by a relative error of at most 0.033.
Values may be sent and summed in bfloat16 or wider, within the bound.
No kernel may reach another device: no remote copies, remote signals or barrier semaphores. Data moves between devices by JAX's collectives and lax.ppermute only.
A program may use at most 64 MiB of HBM per device.

v0:
```python
import jax
import jax.numpy as jnp
from jax import lax
from jax.sharding import PartitionSpec as P

score_scale = 0.07216878364870323
route_scale = 2.5
norm_eps = 1e-06
masked_floor = -1e30


def merged_2(value, axis, join):
    gathered = jax.tree.map(
        lambda a, kind: lax.all_gather(a.astype(kind), axis),
        value,
        (jnp.bfloat16, jnp.bfloat16, jnp.bfloat16),
    )

    def take(source):
        return jax.tree.map(
            lambda a, own: lax.dynamic_index_in_dim(a, source, 0, False).astype(own.dtype),
            gathered,
            value,
        )

    return lax.fori_loop(
        1, lax.axis_size(axis), lambda source, state: join(state, take(source)), take(0)
    )


def join_parts(former, latter):
    top_former, mass_former, weighted_former = former
    top_latter, mass_latter, weighted_latter = latter
    top_both = jnp.maximum(top_former, top_latter)
    factor_former = jnp.exp(top_former - top_both)
    factor_latter = jnp.exp(top_latter - top_both)
    return (
        top_both,
        mass_former * factor_former + mass_latter * factor_latter,
        weighted_former * factor_former[..., None] + weighted_latter * factor_latter[..., None],
    )


def body(
    q_latent,
    q_rope,
    cache_latent,
    cache_rope,
    lengths,
    w_uv,
    w_out,
    resid,
    norm_gain,
    router,
    routes,
    slots,
    w_gateup,
    w_down,
):
    sections = lax.axis_size("sec")
    groups = lax.axis_size("grp")
    members = lax.axis_size("dev")
    section = lax.axis_index("sec")
    row_count, head_total, latent = q_latent.shape
    hist_local = cache_latent.shape[1]
    rope_width = cache_rope.shape[1]
    half_heads = head_total // sections
    head_block = w_uv.shape[0]
    rope_query = q_rope.reshape(row_count, head_total, rope_width)
    scores = (
        jnp.einsum("rhc,rpc->rhp", q_latent, cache_latent, preferred_element_type=jnp.float32)
        + jnp.einsum("rhj,rjp->rhp", rope_query, cache_rope, preferred_element_type=jnp.float32)
    ) * score_scale
    positions = section * hist_local + jnp.arange(hist_local, dtype=jnp.int32)
    usable = (positions[None, :] < lengths[:, None])[:, None, :]
    masked = jnp.where(usable, scores, masked_floor)
    top_score = jnp.max(masked, axis=-1)
    expon = jnp.where(usable, jnp.exp(masked - top_score[..., None]), 0.0)
    mass_sum = jnp.sum(expon, axis=-1)
    weighted = jnp.einsum(
        "rhp,rpc->rhc", expon.astype(jnp.bfloat16), cache_latent, preferred_element_type=jnp.float32
    )
    mine_start = section * half_heads
    merged = merged_2((top_score, mass_sum, weighted), "sec", join_parts)
    top_mine, mass_mine, weighted_mine = [
        lax.dynamic_slice_in_dim(quantity, mine_start, half_heads, 1) for quantity in merged
    ]
    latent_out = (weighted_mine / mass_mine[..., None]).astype(jnp.bfloat16)
    outgoing_heads = latent_out.reshape(row_count, groups, head_block, latent)
    arrived = lax.all_to_all(outgoing_heads, "grp", split_axis=1, concat_axis=0, tiled=True)
    arrived = arrived.reshape(groups * row_count, head_block, latent)
    values = jnp.einsum("nhc,hcv->nhv", arrived, w_uv, preferred_element_type=jnp.float32).astype(
        jnp.bfloat16
    )
    width_heads = head_block * w_uv.shape[2]
    values = values.reshape(groups * row_count, width_heads)
    gathered = lax.all_gather(values, "dev", axis=0, tiled=True)
    natural = gathered.reshape(members, groups, row_count, width_heads).transpose(1, 0, 2, 3)
    natural = natural.reshape(members * groups * row_count, width_heads)
    block_rows = resid.shape[0]
    attention = lax.psum_scatter(
        jnp.dot(natural, w_out, preferred_element_type=jnp.float32).astype(jnp.bfloat16),
        ("sec", "grp"),
        scatter_dimension=0,
        tiled=True,
    ).astype(jnp.float32)
    hidden_state = resid.astype(jnp.float32) + attention
    gained = hidden_state * norm_gain
    square_sum = jnp.sum(hidden_state * hidden_state, axis=-1)
    router_part = jnp.dot(gained, router, precision=lax.Precision.HIGHEST)
    square_total, logit_total = lax.psum((square_sum, router_part), "dev")
    model_width = norm_gain.shape[0] * members
    inverse_rms = lax.rsqrt(square_total / model_width + norm_eps)
    logits = logit_total * inverse_rms[:, None]
    normed = (gained * inverse_rms[:, None]).astype(jnp.bfloat16)
    expert_total = router.shape[1]
    capacity = max(2, 3 * block_rows // 4)
    expert_ids = jnp.arange(expert_total, dtype=jnp.int32)
    chosen_mask = routes[:, :, None] == expert_ids[None, None, :]
    sigmoid_scores = jax.nn.sigmoid(logits)
    picked = jnp.sum(jnp.where(chosen_mask, sigmoid_scores[:, None, :], 0.0), axis=-1)
    route_weight = route_scale * picked / jnp.sum(picked, axis=-1, keepdims=True)
    kept = slots < capacity
    route_weight = jnp.where(kept, route_weight, 0.0)
    slot_index = routes * capacity + slots
    slot_ids = jnp.arange(expert_total * capacity, dtype=jnp.int32)
    placement_matrix = jnp.any(
        (slot_index[:, :, None] == slot_ids[None, None, :]) & kept[:, :, None], axis=1
    ).astype(jnp.bfloat16)
    width_local = normed.shape[1]
    buffer = jnp.einsum("be,bd->ed", placement_matrix, normed, preferred_element_type=jnp.float32)
    buffer = buffer.astype(jnp.bfloat16).reshape(expert_total, capacity, width_local)
    received = lax.all_to_all(buffer, "grp", split_axis=0, concat_axis=1, tiled=True)
    received = lax.all_gather(received, "sec", axis=1, tiled=True)
    incoming_rows = received[0]
    padded_rows = incoming_rows.shape[0]
    gate_weights = w_gateup[0]
    partial_gate = jnp.einsum(
        "pd,dtf->ptf", incoming_rows, gate_weights, preferred_element_type=jnp.float32
    )
    gate_total = lax.psum(partial_gate.astype(jnp.bfloat16), "dev").astype(jnp.float32)
    activated = (jax.nn.silu(gate_total[:, 0]) * gate_total[:, 1]).astype(jnp.bfloat16)
    down_part = jnp.dot(activated, w_down[0], preferred_element_type=jnp.float32)
    down_total = lax.psum_scatter(
        down_part.reshape(sections, padded_rows // sections, width_local).astype(jnp.bfloat16),
        "sec",
        scatter_dimension=0,
        tiled=True,
    )
    expert_rows = down_total.reshape(groups, capacity, width_local)
    returned = lax.all_to_all(expert_rows, "grp", split_axis=0, concat_axis=0, tiled=True)
    returned = returned.reshape(expert_total * capacity, width_local)
    safe_index = jnp.where(kept, slot_index, 0)
    fetched = returned[safe_index]
    mixture = jnp.sum(route_weight[:, :, None] * fetched.astype(jnp.float32), axis=1)
    return (hidden_state + mixture).astype(jnp.bfloat16)


def solution(mesh):
    in_specs = (
        P(("grp", "dev"), None, None),
        P(("grp", "dev"), None),
        P(("grp", "dev"), "sec", None),
        P(("grp", "dev"), None, "sec"),
        P(("grp", "dev")),
        P(("sec", "grp"), None, None),
        P(("sec", "grp"), "dev"),
        P(("sec", "grp"), "dev"),
        P("dev"),
        P("dev", None),
        P(("sec", "grp"), None),
        P(("sec", "grp"), None),
        P("grp", "dev", None, "sec"),
        P("grp", "sec", "dev"),
    )
    out_specs = P(("sec", "grp"), "dev")
    return jax.shard_map(body, mesh=mesh, in_specs=in_specs, out_specs=out_specs, check_vma=False)
```

profile of v0, /device:TPU:1, one launch (start us, length us, event | category | flops | bytes accessed | tf_op | source)
XLA Modules:
  0.0 402.9 jit_solution(10967352460992047660)
XLA Ops:
  7.3 0.9 reduce.5
  8.2 0.1 reshape.317
  8.3 1.1 fusion.23
  9.4 1.9 fusion.46
  11.3 0.2 fusion.12
  11.6 0.4 convolution_convert_fusion.2
  12.0 8.5 %all-gather.3 = bf16[2,1,128]{2,1,0:T(2,128)(2,1)S(1)} all-gather(bf16[1,1,128]{2,1,0:T(2,128)(2,1)S(1)} %convert_bitcast_fusion.1), channel_id=3, replica_groups=mesh['sec'=2,'grp'=16,'dev'=16] {'sec'}, dimensions={0}, use_global_device_ids=true | all-gather | bytes 768 | tf_op jit(solution)/shard_map/all_gather | solution.py:14
  20.4 1.8 all-gather.4
  22.2 0.1 fusion.41
  22.3 0.1 dynamic-slice
  22.4 0.1 dynamic-slice.1
  22.4 2.0 all-gather
  24.5 0.1 fusion.22
  24.6 12.8 %all_to_all.26 = bf16[1,16,4,512]{3,2,0,1:T(4,128)(2,1)S(1)} all-to-all(bf16[1,16,4,512]{3,2,0,1:T(4,128)(2,1)S(1)} %bitcast.106), channel_id=1, replica_groups=mesh['sec'=2,'grp'=16,'dev'=16] {'grp'}, dimensions={1} | all-to-all | bytes 131072 | tf_op jit(solution)/shard_map/all_to_all | solution.py:90
  37.4 0.2 fusion.7
  37.6 32.9 %all_gather.24 = bf16[256,512]{1,0:T(8,128)(2,1)S(1)} all-gather(bf16[16,512]{1,0:T(8,128)(2,1)S(1)} %bitcast.107), channel_id=1, replica_groups=mesh['sec'=2,'grp'=16,'dev'=16] {'dev'}, dimensions={0}, use_global_device_ids=true | all-gather | bytes 278528 | tf_op jit(solution)/shard_map/all_gather | solution.py:97
  70.5 0.1 copy.29
  70.6 1.0 convolution_convert_fusion
  71.6 0.0 reduce-scatter.3.cloned.1.call-update
  71.7 0.0 all-reduce.3.cloned.1.call-start
  71.7 92.9 %reduce-scatter.3.cloned.1.call-done = bf16[8,448]{1,0:T(8,128)(2,1)} async-done(((bf16[256,448]{1,0:T(8,128)(2,1)}), bf16[8,448]{1,0:T(8,128)(2,1)}) %reduce-scatter.3.cloned.1.call-update) | async-done | bytes 7184 | tf_op jit(solution)/shard_map/reduce_scatter | solution.py:101
  164.7 0.8 fusion.30
  165.5 0.8 multiply_reduce_fusion
  166.3 28.1 %all-reduce = (f32[8]{0:T(128)S(1)}, f32[8,16]{1,0:T(8,128)S(1)}) all-reduce(f32[8]{0:T(128)S(1)} %multiply_reduce_fusion, f32[8,16]{1,0:T(8,128)S(1)} %fusion.30), channel_id=1, replica_groups=mesh['sec'=2,'grp'=16,'dev'=16] {'dev'}, use_global_device_ids=true, to_apply=%region_5.6 | all-reduce | flops 136 | bytes 1088 | tf_op jit(solution)/shard_map/psum | solution.py:111
  194.5 0.1 add_divide_fusion
  194.6 0.2 select_reduce_fusion
  194.8 0.1 divide_select_fusion
  194.9 0.1 fusion.29
  195.0 1.0 convolution_convert_fusion.3
  195.9 0.1 reshape.324
  196.0 14.3 %all_to_all.27 = bf16[16,6,448]{2,1,0:T(8,128)(2,1)S(1)} all-to-all(bf16[16,6,448]{2,1,0:T(8,128)(2,1)S(1)} %reshape.324), channel_id=1, replica_groups=mesh['sec'=2,'grp'=16,'dev'=16] {'grp'}, dimensions={0} | all-to-all | bytes 172032 | tf_op jit(solution)/shard_map/all_to_all | solution.py:133
  210.3 0.1 all_to_all.10
  210.4 13.1 %all_gather.25 = bf16[1,192,448]{2,1,0:T(8,128)(2,1)S(1)} all-gather(bf16[1,96,448]{2,1,0:T(8,128)(2,1)S(1)} %all_to_all.10), channel_id=1, replica_groups=mesh['sec'=2,'grp'=16,'dev'=16] {'sec'}, dimensions={1}, use_global_device_ids=true | all-gather | bytes 258048 | tf_op jit(solution)/shard_map/all_gather | solution.py:134
  223.5 1.7 fusion.2
  225.2 0.0 reduce-scatter.5.cloned.1.call-start
  225.3 122.5 %all-reduce.3.cloned.1.call-done = bf16[192,2,1024]{2,0,1:T(8,128)(2,1)} async-done(((bf16[192,2,1024]{2,0,1:T(8,128)(2,1)}), bf16[192,2,1024]{2,0,1:T(8,128)(2,1)}) %all-reduce.3.cloned.1.call-update) | async-done | bytes 786448 | tf_op jit(solution)/shard_map/psum | solution.py:141
  347.8 1.3 convert_element_type.231
  349.1 0.2 fusion.11
  349.4 1.1 convolution_convert_fusion.1
  350.5 25.5 %reduce-scatter.5.cloned.1.call-done = bf16[1,96,448]{2,1,0:T(8,128)(2,1)} async-done(((bf16[2,96,448]{2,1,0:T(8,128)(2,1)}), bf16[1,96,448]{2,1,0:T(8,128)(2,1)}) %reduce-scatter.5.cloned.1.call-update) | async-done | bytes 86032 | tf_op jit(solution)/shard_map/reduce_scatter | solution.py:144
  376.0 1.6 reshape.325
  377.5 8.0 %all-to-all-start.2 = ((bf16[16,6,448]{2,1,0:T(8,128)(2,1)}), bf16[16,6,448]{2,1,0:T(8,128)(2,1)S(1)}, u32[]{:S(2)}, u32[]{:S(2)}) async-start(bf16[16,6,448]{2,1,0:T(8,128)(2,1)} %reshape.325), calls=%async_computation.4 | async-start | bytes 262144 | tf_op jit(solution)/shard_map/all_to_all | solution.py:151
  385.5 0.1 reshape.337
  385.6 9.2 %all-to-all-done.2 = bf16[16,6,448]{2,1,0:T(8,128)(2,1)S(1)} async-done(((bf16[16,6,448]{2,1,0:T(8,128)(2,1)}), bf16[16,6,448]{2,1,0:T(8,128)(2,1)S(1)}, u32[]{:S(2)}, u32[]{:S(2)}) %all-to-all-start.2) | async-done | bytes 86048 | tf_op jit(solution)/shard_map/all_to_all | solution.py:151
  394.9 0.1 reshape.326
  394.9 0.7 gather_fusion
  395.6 0.1 fusion.19
  395.8 0.6 add_convert_fusion
  (35 shorter events, 0.2 us)
Async XLA Ops:
  6.5 217.0 %copy-start = (bf16[1,448,2,1024]{3,2,1,0:T(2,128)(2,1)S(1)}, bf16[1,448,2,1024]{3,2,1,0:T(2,128)(2,1)}, u32[]{:S(2)}) copy-start(bf16[1,448,2,1024]{3,2,1,0:T(2,128)(2,1)} %param.26) | copy-start | bytes 5505028
  6.5 5.0 %copy-start.1 = (bf16[1,1024,512]{2,1,0:T(8,128)(2,1)S(1)}, bf16[1,1024,512]{2,1,0:T(8,128)(2,1)}, u32[]{:S(2)}) copy-start(bf16[1,1024,512]{2,1,0:T(8,128)(2,1)} %param.16) | copy-start | bytes 3145732
  6.5 158.1 %reduce-scatter.3.cloned.1.call-start = ((), (), s32[]{:S(2)}) async-start(), calls=%async_computation.5 | async-start | bytes 270336 | tf_op jit(solution)/shard_map/reduce_scatter | solution.py:101
  11.3 26.1 %copy-start.3 = (bf16[4,512,128]{2,1,0:T(8,128)(2,1)S(1)}, bf16[4,512,128]{2,1,0:T(8,128)(2,1)}, u32[]{:S(2)}) copy-start(bf16[4,512,128]{2,1,0:T(8,128)(2,1)} %param.19) | copy-start | bytes 1572868
  11.9 58.7 %copy-start.4 = (bf16[512,448]{0,1:T(8,128)(2,1)S(1)}, bf16[512,448]{0,1:T(8,128)(2,1)}, u32[]{:S(2)}) copy-start(bf16[512,448]{0,1:T(8,128)(2,1)} %param.20) | copy-start | bytes 1376260
  24.4 140.2 %copy-start.5 = (bf16[8,448]{1,0:T(8,128)(2,1)S(1)}, bf16[8,448]{1,0:T(8,128)(2,1)}, u32[]{:S(2)}) copy-start(bf16[8,448]{1,0:T(8,128)(2,1)} %param.21) | copy-start | bytes 21508
  24.4 140.2 %copy-start.7 = (f32[448,16]{0,1:T(8,128)S(1)}, f32[448,16]{0,1:T(8,128)}, u32[]{:S(2)}) copy-start(f32[448,16]{0,1:T(8,128)} %param.23) | copy-start | bytes 86020
  24.4 140.2 %copy-start.10 = (f32[448]{0:T(512)S(1)}, f32[448]{0:T(512)}, u32[]{:S(2)}) copy-start(f32[448]{0:T(512)} %param.22) | copy-start | bytes 5380
  24.4 170.1 %copy-start.8 = (s32[8,8]{1,0:T(8,128)S(1)}, s32[8,8]{1,0:T(8,128)}, u32[]{:S(2)}) copy-start(s32[8,8]{1,0:T(8,128)} %param.24) | copy-start | bytes 772
  24.4 170.3 %copy-start.9 = (s32[8,8]{1,0:T(8,128)S(1)}, s32[8,8]{1,0:T(8,128)}, u32[]{:S(2)}) copy-start(s32[8,8]{1,0:T(8,128)} %param.25) | copy-start | bytes 772
  71.7 276.1 %all-reduce.3.cloned.1.call-start = ((), (), s32[]{:S(2)}) async-start(), calls=%async_computation.6 | async-start | bytes 1572864 | tf_op jit(solution)/shard_map/psum | solution.py:141
  225.2 124.1 %copy-start.2 = (bf16[1,1024,448]{1,2,0:T(8,128)(2,1)S(1)}, bf16[1,1024,448]{1,2,0:T(8,128)(2,1)}, u32[]{:S(2)}) copy-start(bf16[1,1024,448]{1,2,0:T(8,128)(2,1)} %param.27) | copy-start | bytes 2752516
  225.2 150.8 %reduce-scatter.5.cloned.1.call-start = ((), (), s32[]{:S(2)}) async-start(), calls=%async_computation.7 | async-start | bytes 294912 | tf_op jit(solution)/shard_map/reduce_scatter | solution.py:144
  349.3 46.4 %copy-start.6 = (bf16[8,448]{1,0:T(8,128)(2,1)S(1)}, bf16[8,448]{1,0:T(8,128)(2,1)}, u32[]{:S(2)}) copy-start(bf16[8,448]{1,0:T(8,128)(2,1)} %reduce-scatter.3.cloned.1.call-done) | copy-start | bytes 21508
  377.5 17.3 %all-to-all-start.2 = ((bf16[16,6,448]{2,1,0:T(8,128)(2,1)}), bf16[16,6,448]{2,1,0:T(8,128)(2,1)S(1)}, u32[]{:S(2)}, u32[]{:S(2)}) async-start(bf16[16,6,448]{2,1,0:T(8,128)(2,1)} %reshape.325), calls=%async_computation.4 | async-start | bytes 262144 | tf_op jit(solution)/shard_map/all_to_all | solution.py:151
Sparse Core Ops, SparseCore 0:
  71.8 92.8 reduce-scatter.2
  225.3 122.4 all-reduce.2
  350.8 25.1 reduce-scatter.4
where the time goes:
time: 404 us; the launch traced here: 403 us
  waiting for transfers between devices  250 us (62%)
  blocking collectives  113 us (28%)
  between operations  14.1 us (3%)
  matrix products  9.13 us (2%)
  starting transfers between devices  8.08 us (2%)
  other arithmetic  4.83 us (1%)
    psum x1, waiting for transfers between devices, body(): lax.psum(partial_gate.astype(jnp.bfloat16), 'dev').astype(jnp.float32)  123 us
    reduce_scatter x1, waiting for transfers between devices, body(): lax.psum_scatter(jnp.dot(natural, w_out, preferred_element_type=jnp.float...  92.9 us
    all_gather x1, blocking collectives, body(): gathered = lax.all_gather(values, 'dev', axis=0, tiled=True)  32.9 us
    psum x1, blocking collectives, body(): square_total, logit_total = lax.psum((square_sum, router_part), 'dev')  28.1 us
    reduce_scatter x1, waiting for transfers between devices, body(): lax.psum_scatter(down_part.reshape(sections, padded_rows // sections, wid...  25.5 us
    all_to_all x1, blocking collectives, body(): lax.all_to_all(buffer, 'grp', split_axis=0, concat_axis=1, tiled=True)  14.3 us
    all_gather x1, blocking collectives, body(): received = lax.all_gather(received, 'sec', axis=1, tiled=True)  13.1 us
    all_to_all x1, blocking collectives, body(): lax.all_to_all(outgoing_heads, 'grp', split_axis=1, concat_axis=0, tiled=...  12.8 us
  transfers between devices with their start and end apart: 4, of which 4 were waited for; matrix products, arithmetic and copies ran while one was open for 0% of the time, Pallas kernels for 0%

commit v1 on v0

--- a/solution.py
+++ b/solution.py
@@ -87,7 +87,12 @@
     ]
     latent_out = (weighted_mine / mass_mine[..., None]).astype(jnp.bfloat16)
     outgoing_heads = latent_out.reshape(row_count, groups, head_block, latent)
-    arrived = lax.all_to_all(outgoing_heads, "grp", split_axis=1, concat_axis=0, tiled=True)
+    arrived = jnp.concatenate(
+        lax.all_to_all(
+            jnp.stack(jnp.split(outgoing_heads, lax.axis_size("grp"), axis=1)), "grp", 0, 0
+        ),
+        axis=0,
+    )
     arrived = arrived.reshape(groups * row_count, head_block, latent)
     values = jnp.einsum("nhc,hcv->nhv", arrived, w_uv, preferred_element_type=jnp.float32).astype(
         jnp.bfloat16

time: 404 us -> 404 us (level)
  no operation moved by 1% of the time
where the time goes in v1:
time: 404 us; the launch traced here: 403 us
  waiting for transfers between devices  250 us (62%)
  blocking collectives  113 us (28%)
  between operations  14.2 us (4%)
  matrix products  9.13 us (2%)
  starting transfers between devices  8.08 us (2%)
  other arithmetic  4.83 us (1%)
    psum x1, waiting for transfers between devices, body(): lax.psum(partial_gate.astype(jnp.bfloat16), 'dev').astype(jnp.float32)  122 us
    reduce_scatter x1, waiting for transfers between devices, body(): lax.psum_scatter(jnp.dot(natural, w_out, preferred_element_type=jnp.float...  92.9 us
    all_gather x1, blocking collectives, body(): gathered = lax.all_gather(values, 'dev', axis=0, tiled=True)  32.9 us
    psum x1, blocking collectives, body(): square_total, logit_total = lax.psum((square_sum, router_part), 'dev')  28.2 us
    reduce_scatter x1, waiting for transfers between devices, body(): lax.psum_scatter(down_part.reshape(sections, padded_rows // sections, wid...  25.5 us
    all_to_all x1, blocking collectives, body(): lax.all_to_all(buffer, 'grp', split_axis=0, concat_axis=1, tiled=True)  14.3 us
    all_gather x1, blocking collectives, body(): received = lax.all_gather(received, 'sec', axis=1, tiled=True)  13.1 us
    all_to_all x1, blocking collectives, body(): lax.all_to_all(jnp.stack(jnp.split(outgoing_heads, lax.axis_size('grp'),...  12.8 us
  transfers between devices with their start and end apart: 4, of which 4 were waited for; matrix products, arithmetic and copies ran while one was open for 0% of the time, Pallas kernels for 0%

profile of v1, /device:TPU:1, one launch (start us, length us, event | category | flops | bytes accessed | tf_op | source)
XLA Modules:
  0.0 403.0 jit_solution(9593500738932454487)
XLA Ops:
  7.3 0.9 reduce.5
  8.2 0.1 reshape.310
  8.3 1.1 fusion.23
  9.4 1.9 fusion.46
  11.3 0.2 fusion.12
  11.6 0.4 convolution_convert_fusion.2
  12.0 8.5 %all-gather.3 = bf16[2,1,128]{2,1,0:T(2,128)(2,1)S(1)} all-gather(bf16[1,1,128]{2,1,0:T(2,128)(2,1)S(1)} %convert_bitcast_fusion.1), channel_id=3, replica_groups=mesh['sec'=2,'grp'=16,'dev'=16] {'sec'}, dimensions={0}, use_global_device_ids=true | all-gather | bytes 768 | tf_op jit(solution)/shard_map/all_gather | solution.py:14
  20.4 1.8 all-gather.4
  22.2 0.1 fusion.41
  22.3 0.1 dynamic-slice
  22.4 0.1 dynamic-slice.1
  22.4 2.0 all-gather
  24.5 0.1 fusion.22
  24.9 12.8 %all_to_all.22 = bf16[16,1,1,4,512]{4,3,2,1,0:T(4,128)(2,1)S(1)} all-to-all(bf16[16,1,1,4,512]{4,3,2,1,0:T(4,128)(2,1)S(1)} %constant_dynamic-update-slice_fusion), channel_id=1, replica_groups=mesh['sec'=2,'grp'=16,'dev'=16] {'grp'}, dimensions={0} | all-to-all | bytes 131072 | tf_op jit(solution)/shard_map/all_to_all | solution.py:91
  37.6 0.2 fusion.7
  37.8 32.9 %all_gather.24 = bf16[256,512]{1,0:T(8,128)(2,1)S(1)} all-gather(bf16[16,512]{1,0:T(8,128)(2,1)S(1)} %bitcast.169), channel_id=1, replica_groups=mesh['sec'=2,'grp'=16,'dev'=16] {'dev'}, dimensions={0}, use_global_device_ids=true | all-gather | bytes 278528 | tf_op jit(solution)/shard_map/all_gather | solution.py:102
  70.7 0.1 copy.326
  70.9 1.0 convolution_convert_fusion
  71.9 0.0 reduce-scatter.3.cloned.1.call-update
  71.9 0.0 all-reduce.3.cloned.1.call-start
  72.0 92.9 %reduce-scatter.3.cloned.1.call-done = bf16[8,448]{1,0:T(8,128)(2,1)} async-done(((bf16[256,448]{1,0:T(8,128)(2,1)}), bf16[8,448]{1,0:T(8,128)(2,1)}) %reduce-scatter.3.cloned.1.call-update) | async-done | bytes 7184 | tf_op jit(solution)/shard_map/reduce_scatter | solution.py:106
  164.8 0.8 fusion.30
  165.7 0.8 multiply_reduce_fusion
  166.5 28.2 %all-reduce = (f32[8]{0:T(128)S(1)}, f32[8,16]{1,0:T(8,128)S(1)}) all-reduce(f32[8]{0:T(128)S(1)} %multiply_reduce_fusion, f32[8,16]{1,0:T(8,128)S(1)} %fusion.30), channel_id=1, replica_groups=mesh['sec'=2,'grp'=16,'dev'=16] {'dev'}, use_global_device_ids=true, to_apply=%region_5.6 | all-reduce | flops 136 | bytes 1088 | tf_op jit(solution)/shard_map/psum | solution.py:116
  194.7 0.1 add_divide_fusion
  194.8 0.2 select_reduce_fusion
  195.0 0.1 divide_select_fusion
  195.1 0.1 fusion.29
  195.2 1.0 convolution_convert_fusion.3
  196.1 0.1 reshape.316
  196.2 14.3 %all_to_all.23 = bf16[16,6,448]{2,1,0:T(8,128)(2,1)S(1)} all-to-all(bf16[16,6,448]{2,1,0:T(8,128)(2,1)S(1)} %reshape.316), channel_id=1, replica_groups=mesh['sec'=2,'grp'=16,'dev'=16] {'grp'}, dimensions={0} | all-to-all | bytes 172032 | tf_op jit(solution)/shard_map/all_to_all | solution.py:138
  210.5 0.1 all_to_all.17
  210.6 13.1 %all_gather.25 = bf16[1,192,448]{2,1,0:T(8,128)(2,1)S(1)} all-gather(bf16[1,96,448]{2,1,0:T(8,128)(2,1)S(1)} %all_to_all.17), channel_id=1, replica_groups=mesh['sec'=2,'grp'=16,'dev'=16] {'sec'}, dimensions={1}, use_global_device_ids=true | all-gather | bytes 258048 | tf_op jit(solution)/shard_map/all_gather | solution.py:139
  223.7 1.7 fusion.2
  225.4 0.0 reduce-scatter.5.cloned.1.call-start
  225.5 122.4 %all-reduce.3.cloned.1.call-done = bf16[192,2,1024]{2,0,1:T(8,128)(2,1)} async-done(((bf16[192,2,1024]{2,0,1:T(8,128)(2,1)}), bf16[192,2,1024]{2,0,1:T(8,128)(2,1)}) %all-reduce.3.cloned.1.call-update) | async-done | bytes 786448 | tf_op jit(solution)/shard_map/psum | solution.py:146
  347.9 1.3 convert_element_type.231
  349.2 0.2 fusion.11
  349.5 1.1 convolution_convert_fusion.1
  350.6 25.5 %reduce-scatter.5.cloned.1.call-done = bf16[1,96,448]{2,1,0:T(8,128)(2,1)} async-done(((bf16[2,96,448]{2,1,0:T(8,128)(2,1)}), bf16[1,96,448]{2,1,0:T(8,128)(2,1)}) %reduce-scatter.5.cloned.1.call-update) | async-done | bytes 86032 | tf_op jit(solution)/shard_map/reduce_scatter | solution.py:149
  376.1 1.6 reshape.317
  377.7 8.0 %all-to-all-start.2 = ((bf16[16,6,448]{2,1,0:T(8,128)(2,1)}), bf16[16,6,448]{2,1,0:T(8,128)(2,1)S(1)}, u32[]{:S(2)}, u32[]{:S(2)}) async-start(bf16[16,6,448]{2,1,0:T(8,128)(2,1)} %reshape.317), calls=%async_computation.4 | async-start | bytes 262144 | tf_op jit(solution)/shard_map/all_to_all | solution.py:156
  385.7 0.1 reshape.329
  385.8 9.2 %all-to-all-done.2 = bf16[16,6,448]{2,1,0:T(8,128)(2,1)S(1)} async-done(((bf16[16,6,448]{2,1,0:T(8,128)(2,1)}), bf16[16,6,448]{2,1,0:T(8,128)(2,1)S(1)}, u32[]{:S(2)}, u32[]{:S(2)}) %all-to-all-start.2) | async-done | bytes 86048 | tf_op jit(solution)/shard_map/all_to_all | solution.py:156
  395.0 0.1 reshape.318
  395.0 0.7 gather_fusion
  395.8 0.1 fusion.19
  395.9 0.6 add_convert_fusion
  (51 shorter events, 0.4 us)
Async XLA Ops:
  6.5 217.2 %copy-start = (bf16[1,448,2,1024]{3,2,1,0:T(2,128)(2,1)S(1)}, bf16[1,448,2,1024]{3,2,1,0:T(2,128)(2,1)}, u32[]{:S(2)}) copy-start(bf16[1,448,2,1024]{3,2,1,0:T(2,128)(2,1)} %param.26) | copy-start | bytes 5505028
  6.5 5.0 %copy-start.1 = (bf16[1,1024,512]{2,1,0:T(8,128)(2,1)S(1)}, bf16[1,1024,512]{2,1,0:T(8,128)(2,1)}, u32[]{:S(2)}) copy-start(bf16[1,1024,512]{2,1,0:T(8,128)(2,1)} %param.16) | copy-start | bytes 3145732
  6.5 158.3 %reduce-scatter.3.cloned.1.call-start = ((), (), s32[]{:S(2)}) async-start(), calls=%async_computation.5 | async-start | bytes 270336 | tf_op jit(solution)/shard_map/reduce_scatter | solution.py:106
  11.3 26.3 %copy-start.3 = (bf16[4,512,128]{2,1,0:T(8,128)(2,1)S(1)}, bf16[4,512,128]{2,1,0:T(8,128)(2,1)}, u32[]{:S(2)}) copy-start(bf16[4,512,128]{2,1,0:T(8,128)(2,1)} %param.19) | copy-start | bytes 1572868
  11.9 58.9 %copy-start.4 = (bf16[512,448]{0,1:T(8,128)(2,1)S(1)}, bf16[512,448]{0,1:T(8,128)(2,1)}, u32[]{:S(2)}) copy-start(bf16[512,448]{0,1:T(8,128)(2,1)} %param.20) | copy-start | bytes 1376260
  24.4 140.4 %copy-start.5 = (bf16[8,448]{1,0:T(8,128)(2,1)S(1)}, bf16[8,448]{1,0:T(8,128)(2,1)}, u32[]{:S(2)}) copy-start(bf16[8,448]{1,0:T(8,128)(2,1)} %param.21) | copy-start | bytes 21508
  24.4 140.4 %copy-start.7 = (f32[448,16]{0,1:T(8,128)S(1)}, f32[448,16]{0,1:T(8,128)}, u32[]{:S(2)}) copy-start(f32[448,16]{0,1:T(8,128)} %param.23) | copy-start | bytes 86020
  24.4 140.4 %copy-start.10 = (f32[448]{0:T(512)S(1)}, f32[448]{0:T(512)}, u32[]{:S(2)}) copy-start(f32[448]{0:T(512)} %param.22) | copy-start | bytes 5380
  24.4 170.3 %copy-start.8 = (s32[8,8]{1,0:T(8,128)S(1)}, s32[8,8]{1,0:T(8,128)}, u32[]{:S(2)}) copy-start(s32[8,8]{1,0:T(8,128)} %param.24) | copy-start | bytes 772
  24.4 170.5 %copy-start.9 = (s32[8,8]{1,0:T(8,128)S(1)}, s32[8,8]{1,0:T(8,128)}, u32[]{:S(2)}) copy-start(s32[8,8]{1,0:T(8,128)} %param.25) | copy-start | bytes 772
  71.9 276.0 %all-reduce.3.cloned.1.call-start = ((), (), s32[]{:S(2)}) async-start(), calls=%async_computation.6 | async-start | bytes 1572864 | tf_op jit(solution)/shard_map/psum | solution.py:146
  225.4 124.1 %copy-start.2 = (bf16[1,1024,448]{1,2,0:T(8,128)(2,1)S(1)}, bf16[1,1024,448]{1,2,0:T(8,128)(2,1)}, u32[]{:S(2)}) copy-start(bf16[1,1024,448]{1,2,0:T(8,128)(2,1)} %param.27) | copy-start | bytes 2752516
  225.4 150.7 %reduce-scatter.5.cloned.1.call-start = ((), (), s32[]{:S(2)}) async-start(), calls=%async_computation.7 | async-start | bytes 294912 | tf_op jit(solution)/shard_map/reduce_scatter | solution.py:149
  349.5 46.4 %copy-start.6 = (bf16[8,448]{1,0:T(8,128)(2,1)S(1)}, bf16[8,448]{1,0:T(8,128)(2,1)}, u32[]{:S(2)}) copy-start(bf16[8,448]{1,0:T(8,128)(2,1)} %reduce-scatter.3.cloned.1.call-done) | copy-start | bytes 21508
  377.7 17.3 %all-to-all-start.2 = ((bf16[16,6,448]{2,1,0:T(8,128)(2,1)}), bf16[16,6,448]{2,1,0:T(8,128)(2,1)S(1)}, u32[]{:S(2)}, u32[]{:S(2)}) async-start(bf16[16,6,448]{2,1,0:T(8,128)(2,1)} %reshape.317), calls=%async_computation.4 | async-start | bytes 262144 | tf_op jit(solution)/shard_map/all_to_all | solution.py:156
Sparse Core Ops, SparseCore 0:
  72.0 92.7 reduce-scatter.2
  225.5 122.3 all-reduce.2
  350.9 25.1 reduce-scatter.4
